TPU v7x, 32 devices: a whole 2x2x4 slice. The times are simulated.
32 devices in a mesh: rep: 2 (over y), grp: 4 (over z), ing: 2 (over x), dp: 2 (over core).
Axes of the slice: x: 2, y: 2, z: 4, core: 2. Of those that a mesh axis runs over, the one named last changes fastest.
Arguments:
- tokens: bfloat16 [8192, 7168], P(('rep', 'grp', 'ing', 'dp')), parts along dimension 0, may hold values from -6 to 6
- routes: int32 [8192, 8], P(('rep', 'grp', 'ing', 'dp')), parts along dimension 0, may hold values from 0 to 255, as said below
- route_gates: float32 [8192, 8], P(('rep', 'grp', 'ing', 'dp')), parts along dimension 0, may hold values from 0.2 to 2.5
- gate_proj: bfloat16 [4, 7168, 1024], P('grp', None, ('ing', 'dp')), may hold values from -0.0625 to 0.0625
- up_proj: bfloat16 [4, 7168, 1024], P('grp', None, ('ing', 'dp')), may hold values from -0.0625 to 0.0625
- down_proj: bfloat16 [4, 1024, 7168], P('grp', ('ing', 'dp')), may hold values from -0.1875 to 0.1875
Outputs:
- moe_out: bfloat16 [8192, 7168], P(('rep', 'grp', 'ing', 'dp')), parts along dimension 0
There are 2 independent parts, one for each index of `rep`. A program takes and returns all parts, laid end to end along the dimension named above; an argument that names none is the same for every part. Nothing has to cross between parts.
Inputs may be any that keep to these rules, and one draw needn't show every extreme that they name: `routes`: the 8 ids of a token are distinct and at most one of them is a multiple of 64. Within the rows of one device no multiple of 64 stands in more than 32 rows, and one such id stands in exactly 32 rows of every device.
All inputs are finite; a program needn't handle non-finite values.
Results may differ from a plain program's by a relative error of at most 0.011.
Values may be sent and summed in bfloat16 or wider, within the bound.
A program may use at most 128 MiB of HBM per device.

v0:
```python
import jax
import jax.numpy as jnp
from jax import lax
from jax.sharding import PartitionSpec as P

EXPERTS = 256


def expert_rows(routed_rows, weight_set):
    gate_weight, up_weight, down_weight = weight_set
    gathered = lax.all_gather(routed_rows, "ing", axis=0, tiled=True)
    gate_act = jnp.dot(gathered, gate_weight[0], preferred_element_type=jnp.float32)
    up_act = jnp.dot(gathered, up_weight[0], preferred_element_type=jnp.float32)
    hidden = (jax.nn.silu(gate_act) * up_act).astype(jnp.bfloat16)
    return lax.psum_scatter(
        jnp.dot(hidden, down_weight[0], preferred_element_type=jnp.float32).astype(jnp.bfloat16),
        "ing",
        scatter_dimension=0,
        tiled=True,
    )


def on_device(tokens, routes, route_gates, gate_proj, up_proj, down_proj):
    groups = lax.axis_size("grp")
    token_count = tokens.shape[0]
    model_width = tokens.shape[1]
    slot_count = token_count // (2 * groups)
    spacing = EXPERTS // groups
    struck = routes % spacing == 0
    owners = jnp.sum(jnp.where(struck, routes // spacing, 0), axis=1)
    landed = jnp.any(struck, axis=1)
    weighting = jnp.sum(jnp.where(struck, route_gates, jnp.zeros_like(route_gates)), axis=1)
    chosen = ((owners[:, None] == jnp.arange(groups)[None, :]) & landed[:, None]).astype(jnp.int32)
    before = jnp.cumsum(chosen, axis=0) - chosen
    ranking = jnp.sum(before * chosen, axis=1)
    target = owners * slot_count + ranking
    placing = (
        (jnp.arange(groups * slot_count)[:, None] == target[None, :]) & landed[None, :]
    ).astype(jnp.bfloat16)
    outgoing = jnp.dot(placing, tokens, preferred_element_type=jnp.float32).astype(jnp.bfloat16)
    outgoing = outgoing.reshape(groups, slot_count, model_width)
    arrived = lax.all_to_all(outgoing, "grp", split_axis=0, concat_axis=0, tiled=True)
    weight_set = (
        lax.all_gather(gate_proj, "dp", axis=2, tiled=True),
        lax.all_gather(up_proj, "dp", axis=2, tiled=True),
        lax.all_gather(down_proj, "dp", axis=1, tiled=True),
    )
    results = expert_rows(arrived.reshape(-1, model_width), weight_set).reshape(
        groups, slot_count, model_width
    )
    returned = lax.all_to_all(results, "grp", split_axis=0, concat_axis=0, tiled=True)
    routed = jnp.einsum(
        "st,sd->td", placing, returned.reshape(-1, model_width), preferred_element_type=jnp.float32
    )
    return (weighting[:, None] * routed).astype(jnp.bfloat16)


def solution(mesh):
    placed = (
        P(("rep", "grp", "ing", "dp"), None),
        P(("rep", "grp", "ing", "dp"), None),
        P(("rep", "grp", "ing", "dp"), None),
        P("grp", None, ("ing", "dp")),
        P("grp", None, ("ing", "dp")),
        P("grp", ("ing", "dp"), None),
    )
    return jax.shard_map(
        on_device,
        mesh=mesh,
        in_specs=placed,
        out_specs=P(("rep", "grp", "ing", "dp"), None),
        check_vma=False,
    )
```

profile of v0, /device:TPU:0, one launch (start us, length us, event | category | flops | bytes accessed | tf_op | source)
XLA Modules:
  0.0 289.9 jit_solution(5550552822195389868)
XLA Ops:
  6.5 0.0 all-gather.5.cloned.1.call-start
  6.5 0.7 select_reduce_fusion
  7.3 0.7 fusion.29
  8.0 1.2 reduce-window.6
  9.2 0.1 slice.8
  9.3 0.1 copy.7
  9.5 0.1 copy.8
  9.6 0.1 add_bitcast_fusion
  9.7 2.7 convolution_convert_fusion.1
  12.4 48.8 %all_to_all.10 = bf16[4,32,7168]{2,1,0:T(8,128)(2,1)} all-to-all(bf16[4,32,7168]{2,1,0:T(8,128)(2,1)S(1)} %bitcast.46), channel_id=1, replica_groups=mesh['rep'=2,'grp'=4,'ing'=2,'dp'=2] {'grp'}, dimensions={0} | all-to-all | bytes 3670016 | tf_op jit(solution)/shard_map/all_to_all | solution.py:42
  61.2 0.0 all-gather.5.cloned.1.call-update
  61.2 0.0 all-gather.7.cloned.1.call-start
  61.2 0.7 all-gather.7.cloned.1.call-update
  62.0 0.0 all-gather.11.cloned.1.call-start
  62.0 0.7 all-gather.11.cloned.1.call-update
  62.7 0.0 all-gather.9.cloned.1.call-start
  62.7 0.5 all-gather.9.cloned.1.call-update
  63.3 0.0 reduce-scatter.2.cloned.1.call-start
  63.3 48.1 %all-gather.5.cloned.1.call-done = bf16[256,7168]{1,0:T(8,128)(2,1)} async-done(((bf16[128,7168]{1,0:T(8,128)(2,1)}), bf16[256,7168]{1,0:T(8,128)(2,1)}) %all-gather.5.cloned.1.call-update) | async-done | bytes 3670032 | tf_op jit(solution)/shard_map/all_gather | solution.py:11
  111.4 18.5 %all-gather.7.cloned.1.call-done = bf16[1,7168,512]{2,1,0:T(8,128)(2,1)} async-done(((bf16[1,7168,256]{2,1,0:T(8,128)(2,1)}), bf16[1,7168,512]{2,1,0:T(8,128)(2,1)}) %all-gather.7.cloned.1.call-update) | async-done | bytes 7340048 | tf_op jit(solution)/shard_map/all_gather | solution.py:44
  129.9 6.2 %fusion.4 = f32[256,512]{1,0:T(8,128)S(1)} fusion(bf16[256,7168]{1,0:T(8,128)(2,1)} %all-gather.5.cloned.1.call-done, bf16[1,7168,512]{2,1,0:T(8,128)(2,1)} %all-gather.7.cloned.1.call-done), kind=kOutput, calls=%fused_computation.7 | convolution fusion | flops 1879048192 | bytes 11534336 | tf_op jit(solution)/shard_map/dot_general | solution.py:12
  136.2 14.8 %all-gather.11.cloned.1.call-done = bf16[1,512,7168]{2,1,0:T(8,128)(2,1)} async-done(((bf16[1,256,7168]{2,1,0:T(8,128)(2,1)}), bf16[1,512,7168]{2,1,0:T(8,128)(2,1)}) %all-gather.11.cloned.1.call-update) | async-done | bytes 7340048 | tf_op jit(solution)/shard_map/all_gather | solution.py:46
  151.0 19.6 %all-gather.9.cloned.1.call-done = bf16[1,7168,512]{2,1,0:T(8,128)(2,1)} async-done(((bf16[1,7168,256]{2,1,0:T(8,128)(2,1)}), bf16[1,7168,512]{2,1,0:T(8,128)(2,1)}) %all-gather.9.cloned.1.call-update) | async-done | bytes 7340048 | tf_op jit(solution)/shard_map/all_gather | solution.py:45
  170.6 12.1 %convolution_convert_fusion = bf16[256,7168]{1,0:T(8,128)(2,1)} fusion(bf16[1,512,7168]{2,1,0:T(8,128)(2,1)} %all-gather.11.cloned.1.call-done, bf16[256,7168]{1,0:T(8,128)(2,1)} %all-gather.5.cloned.1.call-done, bf16[1,7168,512]{2,1,0:T(8,128)(2,1)} %all-gather.9.cloned.1.call-done, f32[256,512]{1,0:T(8,128)S(1)} %fusion.4), kind=kOutput, calls=%fused_computation.2 | convolution fusion | flops 3760717824 | bytes 22544384 | tf_op jit(solution)/shard_map/dot_general | solution.py:16
  182.7 0.0 reduce-scatter.2.cloned.1.call-update
  182.7 50.4 %reduce-scatter.2.cloned.1.call-done = bf16[128,7168]{1,0:T(8,128)(2,1)} async-done(((bf16[256,7168]{1,0:T(8,128)(2,1)}), bf16[128,7168]{1,0:T(8,128)(2,1)}) %reduce-scatter.2.cloned.1.call-update) | async-done | bytes 1835024 | tf_op jit(solution)/shard_map/reduce_scatter | solution.py:15
  233.2 47.2 %all_to_all.11 = bf16[4,32,7168]{2,1,0:T(8,128)(2,1)S(1)} all-to-all(bf16[4,32,7168]{2,1,0:T(8,128)(2,1)} %bitcast.47), channel_id=1, replica_groups=mesh['rep'=2,'grp'=4,'ing'=2,'dp'=2] {'grp'}, dimensions={0} | all-to-all | bytes 3670016 | tf_op jit(solution)/shard_map/all_to_all | solution.py:51
  280.4 3.0 %fusion = bf16[256,7168]{1,0:T(8,128)(2,1)} fusion(bf16[128,7168]{1,0:T(8,128)(2,1)S(1)} %bitcast.45, f32[256]{0:T(256)S(1)} %get-tuple-element.5, s32[256]{0:T(256)S(1)} %multiply_add_fusion, pred[256]{0:T(512)(128)(4,1)S(1)} %reduce_or.9), kind=kOutput, calls=%fused_computation.1 | convolution fusion | flops 473497600 | bytes 5507328 | tf_op jit(solution)/shard_map/st,sd->td/dot_general | solution.py:52
  (6 shorter events, 0.1 us)
Async XLA Ops:
  6.5 104.8 %all-gather.5.cloned.1.call-start = ((), (), s32[]{:S(2)}) async-start(), calls=%async_computation.3 | async-start | bytes 5505024 | tf_op jit(solution)/shard_map/all_gather | solution.py:11
  61.2 68.7 %all-gather.7.cloned.1.call-start = ((), (), s32[]{:S(2)}) async-start(), calls=%async_computation.4 | async-start | bytes 11010048 | tf_op jit(solution)/shard_map/all_gather | solution.py:44
  62.0 89.0 %all-gather.11.cloned.1.call-start = ((), (), s32[]{:S(2)}) async-start(), calls=%async_computation.6 | async-start | bytes 11010048 | tf_op jit(solution)/shard_map/all_gather | solution.py:46
  62.7 107.9 %all-gather.9.cloned.1.call-start = ((), (), s32[]{:S(2)}) async-start(), calls=%async_computation.5 | async-start | bytes 11010048 | tf_op jit(solution)/shard_map/all_gather | solution.py:45
  63.3 169.9 %reduce-scatter.2.cloned.1.call-start = ((), (), s32[]{:S(2)}) async-start(), calls=%async_computation.7 | async-start | bytes 5505024 | tf_op jit(solution)/shard_map/reduce_scatter | solution.py:15
Sparse Core Ops, SparseCore 0:
  61.3 49.9 all-gather.4
  112.9 16.9 all-gather.6
  131.4 19.4 all-gather.10
  152.4 18.1 all-gather.8
  182.8 50.2 reduce-scatter.1
where the time goes:
time: 290 us
  waiting for transfers between devices  153 us (53%)
  blocking collectives  96 us (33%)
  matrix products  24.1 us (8%)
  between operations  13.2 us (5%)
    reduce_scatter x1, waiting for transfers between devices, expert_rows(): lax.psum_scatter(jnp.dot(hidden, down_weight[0], preferred_element_type=j...  50.4 us
    all_to_all x1, blocking collectives, on_device(): lax.all_to_all(outgoing, 'grp', split_axis=0, concat_axis=0, tiled=True)  48.8 us
    all_gather x1, waiting for transfers between devices, expert_rows(): gathered = lax.all_gather(routed_rows, 'ing', axis=0, tiled=True)  48.1 us
    all_to_all x1, blocking collectives, on_device(): lax.all_to_all(results, 'grp', split_axis=0, concat_axis=0, tiled=True)  47.2 us
    all_gather x1, waiting for transfers between devices, on_device(): lax.all_gather(up_proj, 'dp', axis=2, tiled=True)  19.6 us
    all_gather x1, waiting for transfers between devices, on_device(): lax.all_gather(gate_proj, 'dp', axis=2, tiled=True)  18.5 us
    all_gather x1, waiting for transfers between devices, on_device(): lax.all_gather(down_proj, 'dp', axis=1, tiled=True)  14.8 us
    dot_general x1, matrix products, expert_rows(): jnp.dot(hidden, down_weight[0], preferred_element_type=jnp.float32)  12.1 us
  transfers between devices with their start and end apart: 5, of which 5 were waited for; matrix products, arithmetic and copies ran while one was open for 2% of the time, Pallas kernels for 0%

commit v1 on v0

--- a/solution.py
+++ b/solution.py
@@ -1,9 +1,14 @@
+import functools
+
 import jax
 import jax.numpy as jnp
 from jax import lax
+from jax.experimental import pallas as pl
+from jax.experimental.pallas import tpu as pltpu
 from jax.sharding import PartitionSpec as P
 
 EXPERTS = 256
+MESH = pl.DeviceIdType.MESH
 
 
 def expert_rows(routed_rows, weight_set):
@@ -18,6 +23,198 @@
         scatter_dimension=0,
         tiled=True,
     )
+
+
+def swapped(z, d):
+    flipped = z
+    if d % 2:
+        flipped = flipped + 1 - 2 * (z % 2)
+    if d // 2:
+        flipped = flipped + 2 - 4 * ((z // 2) % 2)
+    return flipped
+
+
+def expert_kernel(
+    outgoing, gate_hbm, up_hbm, down_hbm, returned,
+    gate_w, up_w, down_w, rows, kept, leaving, coming, summed,
+    local_sem, weight_send, weight_recv, zin_send, zin_recv, xin_send, xin_recv,
+    xout_send, xout_recv, zout_send, zout_recv,
+):
+    z, x, c = (lax.axis_index(name) for name in ("grp", "ing", "dp"))
+    across, sibling = {"ing": 1 - x}, {"dp": 1 - c}
+    half_rows, width = rows.shape[3], rows.shape[4]
+
+    barrier = pltpu.get_barrier_semaphore()
+    peers = [across, sibling] + [{"grp": swapped(z, d)} for d in (1, 2, 3)]
+    for peer in peers:
+        pl.semaphore_signal(barrier, inc=1, device_id=peer, device_id_type=MESH)
+    pl.semaphore_wait(barrier, len(peers))
+
+    def remote(src, dst, send, recv, to):
+        return pltpu.make_async_remote_copy(
+            src_ref=src, dst_ref=dst, send_sem=send, recv_sem=recv, device_id=to, device_id_type=MESH
+        )
+
+    def zin(d, h):
+        t = swapped(z, d)
+        return remote(outgoing.at[t, h], rows.at[d, h, 0], zin_send.at[d, h], zin_recv.at[d, h], {"grp": t})
+
+    def xin(d, h):
+        return remote(rows.at[d, h, 0], rows.at[d, h, 1], xin_send.at[d, h], xin_recv.at[d, h], across)
+
+    def xout(d, h):
+        return remote(leaving.at[d, h], coming.at[d, h], xout_send.at[d, h], xout_recv.at[d, h], across)
+
+    def zout(d, h, t):
+        return remote(summed.at[d, h], returned.at[z, h], zout_send.at[d, h], zout_recv.at[d, h], {"grp": t})
+
+    def flipped(d):
+        low, high = d % 2, d // 2
+        return z + low * (1 - 2 * (z % 2)) + high * (2 - 4 * ((z // 2) % 2))
+
+    for h in range(2):
+        zin(2, h).start()
+    for h in range(2):
+        rows[0, h, 0] = outgoing[z, h]
+        xin(0, h).start()
+    for h in range(2):
+        zin(1, h).start()
+    weights = []
+    for i, (hbm, vmem) in enumerate(((gate_hbm, gate_w), (up_hbm, up_w), (down_hbm, down_w))):
+        own = pltpu.make_async_copy(hbm, vmem.at[0], local_sem.at[i])
+        other = remote(hbm, vmem.at[1], weight_send.at[i], weight_recv.at[i], sibling)
+        own.start()
+        other.start()
+        weights.append((own, other))
+    for h in range(2):
+        zin(2, h).wait_recv()
+        xin(2, h).start()
+        zin(3, h).start()
+    for h in range(2):
+        zin(1, h).wait_recv()
+        xin(1, h).start()
+    for own, other in weights[:2]:
+        own.wait()
+        other.wait_recv()
+
+    def chunk_of(i):
+        pair = i // 2
+        return 2 * (1 - pair % 2) + pair // 2, i % 2
+
+    def finish(i):
+        d, h = chunk_of(i)
+        xout(d, h).wait_recv()
+        summed[d, h] = (kept[d, h] + coming[d, h].astype(jnp.float32)).astype(jnp.bfloat16)
+
+        @pl.when(d == 0)
+        def _():
+            pltpu.make_async_copy(summed.at[d, h], returned.at[z, h], local_sem.at[3 + h]).start()
+
+        @pl.when(d != 0)
+        def _():
+            zout(d, h, flipped(d)).start()
+
+    def compute(i, carry):
+        d, h = chunk_of(i)
+        xin(d, h).wait_recv()
+        chunk = rows.at[d, h]
+        tile = chunk[...].reshape(2 * half_rows, width)
+        hidden = []
+        for w in range(2):
+            gate_act = jnp.dot(tile, gate_w[w], preferred_element_type=jnp.float32)
+            up_act = jnp.dot(tile, up_w[w], preferred_element_type=jnp.float32)
+            hidden.append((gate_act / (1.0 + jnp.exp(-gate_act)) * up_act).astype(jnp.bfloat16))
+
+        @pl.when(i == 0)
+        def _():
+            weights[2][0].wait()
+            weights[2][1].wait_recv()
+
+        step = 1024
+
+        def down(n, carry):
+            columns = pl.ds(pl.multiple_of(n * step, step), step)
+            part = jnp.dot(hidden[0], down_w[0, :, columns], preferred_element_type=jnp.float32)
+            part += jnp.dot(hidden[1], down_w[1, :, columns], preferred_element_type=jnp.float32)
+            kept[d, h, :, columns] = part[:half_rows]
+            leaving[d, h, :, columns] = part[half_rows:].astype(jnp.bfloat16)
+            return carry
+
+        lax.fori_loop(0, width // step, down, 0)
+        xout(d, h).start()
+
+        @pl.when((i == 1) | (i == 3))
+        def _():
+            zin(3, i // 2).wait_recv()
+            xin(3, i // 2).start()
+
+        @pl.when(i >= 2)
+        def _():
+            finish(i - 2)
+
+        return carry
+
+    lax.fori_loop(0, 8, compute, 0)
+    for i in (6, 7):
+        finish(i)
+    for own, other in weights:
+        other.wait_send()
+    for h in range(2):
+        pltpu.make_async_copy(summed.at[0, h], returned.at[z, h], local_sem.at[3 + h]).wait()
+        for d in range(4):
+            xin(d, h).wait_send()
+            xout(d, h).wait_send()
+            if d:
+                zin(d, h).wait_send()
+                zout(d, h, swapped(z, d)).wait()
+
+
+def expert_call(outgoing, gate_proj, up_proj, down_proj):
+    groups, slot_count, model_width = outgoing.shape
+    hidden = gate_proj.shape[2]
+    halves = (groups, 2, slot_count // 2, model_width)
+    dma = pltpu.SemaphoreType.DMA
+    vmem, hbm = pl.BlockSpec(memory_space=pltpu.VMEM), pl.BlockSpec(memory_space=pl.ANY)
+    bf16, f32 = jnp.bfloat16, jnp.float32
+    returned = pl.pallas_call(
+        expert_kernel,
+        out_shape=jax.ShapeDtypeStruct(halves, bf16),
+        in_specs=[vmem, hbm, hbm, hbm],
+        out_specs=hbm,
+        scratch_shapes=[
+            pltpu.VMEM((2, model_width, hidden), bf16),
+            pltpu.VMEM((2, model_width, hidden), bf16),
+            pltpu.VMEM((2, hidden, model_width), bf16),
+            pltpu.VMEM((groups, 2, 2, slot_count // 2, model_width), bf16),
+            pltpu.VMEM(halves, f32),
+            pltpu.VMEM(halves, bf16),
+            pltpu.VMEM(halves, bf16),
+            pltpu.VMEM(halves, bf16),
+            dma((5,)),
+            dma((3,)),
+            dma((3,)),
+        ]
+        + [dma((groups, 2))] * 8,
+        compiler_params=pltpu.CompilerParams(
+            collective_id=0, has_side_effects=True, vmem_limit_bytes=56 * 2**20
+        ),
+        name="routed_experts",
+    )(outgoing.reshape(halves), gate_proj[0], up_proj[0], down_proj[0])
+    return returned.reshape(groups, slot_count, model_width)
+
+
+def plain_call(outgoing, gate_proj, up_proj, down_proj):
+    groups, slot_count, model_width = outgoing.shape
+    arrived = lax.all_to_all(outgoing, "grp", split_axis=0, concat_axis=0, tiled=True)
+    weight_set = (
+        lax.all_gather(gate_proj, "dp", axis=2, tiled=True),
+        lax.all_gather(up_proj, "dp", axis=2, tiled=True),
+        lax.all_gather(down_proj, "dp", axis=1, tiled=True),
+    )
+    results = expert_rows(arrived.reshape(-1, model_width), weight_set).reshape(
+        groups, slot_count, model_width
+    )
+    return lax.all_to_all(results, "grp", split_axis=0, concat_axis=0, tiled=True)
 
 
 def on_device(tokens, routes, route_gates, gate_proj, up_proj, down_proj):
@@ -39,16 +236,10 @@
     ).astype(jnp.bfloat16)
     outgoing = jnp.dot(placing, tokens, preferred_element_type=jnp.float32).astype(jnp.bfloat16)
     outgoing = outgoing.reshape(groups, slot_count, model_width)
-    arrived = lax.all_to_all(outgoing, "grp", split_axis=0, concat_axis=0, tiled=True)
-    weight_set = (
-        lax.all_gather(gate_proj, "dp", axis=2, tiled=True),
-        lax.all_gather(up_proj, "dp", axis=2, tiled=True),
-        lax.all_gather(down_proj, "dp", axis=1, tiled=True),
-    )
-    results = expert_rows(arrived.reshape(-1, model_width), weight_set).reshape(
-        groups, slot_count, model_width
-    )
-    returned = lax.all_to_all(results, "grp", split_axis=0, concat_axis=0, tiled=True)
+    if groups == 4 and lax.axis_size("ing") == 2 and lax.axis_size("dp") == 2 and slot_count == 32:
+        returned = expert_call(outgoing, gate_proj, up_proj, down_proj)
+    else:
+        returned = plain_call(outgoing, gate_proj, up_proj, down_proj)
     routed = jnp.einsum(
         "st,sd->td", placing, returned.reshape(-1, model_width), preferred_element_type=jnp.float32
     )

time: 290 us -> 115 us (0.40)
  waiting for transfers between devices: 153 us -> 0 us
  Pallas kernels: 0 us -> 104 us
  blocking collectives: 96 us -> 0 us
  matrix products: 24.1 us -> 8.42 us
  between operations: 13.2 us -> 0.02 us
    pallas_call x0 -> x1, Pallas kernels: none -> 104 us  [expert_call(): pl.pallas_call(expert_kernel, out_shape=jax.ShapeDtypeStruct(halves, bf16...]
    all_gather x4 -> x0, waiting for transfers between devices: 101 us -> none  [the longest x1 48.1 us: expert_rows(): gathered = lax.all_gather(routed_rows, 'ing', axis=0, tiled=True)]
    all_to_all x2 -> x0, blocking collectives: 96 us -> none  [the longest x1 48.8 us: on_device(): lax.all_to_all(outgoing, 'grp', split_axis=0, concat_axis=0, tiled=True)]
    reduce_scatter x1 -> x0, waiting for transfers between devices: 50.4 us -> none  [expert_rows(): lax.psum_scatter(jnp.dot(hidden, down_weight[0], preferred_element_type=j...]
    dot_general x2 -> x0, matrix products: 18.4 us -> none  [the longest x1 12.1 us: expert_rows(): jnp.dot(hidden, down_weight[0], preferred_element_type=jnp.float32)]
  transfers between devices with their start and end apart: 5 -> 0, of which waited for: 5 -> 0; matrix products, arithmetic and copies ran while one was open for 2% -> 0% of each run, Pallas kernels for 0% -> 0%
where the time goes in v1:
time: 115 us
  Pallas kernels  104 us (90%)
  matrix products  8.42 us (7%)
  other arithmetic  2.85 us (2%)
    pallas_call x1, Pallas kernels, expert_call(): pl.pallas_call(expert_kernel, out_shape=jax.ShapeDtypeStruct(halves, bf16...  104 us
    dot_general x1, matrix products, on_device(): jnp.einsum('st,sd->td', placing, returned.reshape(-1, model_width), prefe...  4.5 us
    dot_general x1, matrix products, on_device(): jnp.dot(placing, tokens, preferred_element_type=jnp.float32)  3.92 us

profile of v1, /device:TPU:0, one launch (start us, length us, event | category | flops | bytes accessed | tf_op | source)
XLA Modules:
  0.0 115.2 jit_solution(8976905450850046956)
XLA Ops:
  0.0 0.7 select_reduce_fusion
  0.8 0.7 fusion.10
  1.5 1.2 %reduce-window.6 = s32[4,2,128]{2,1,0:T(2,128)S(1)} reduce-window(s32[4,2,128]{2,1,0:T(2,128)S(1)} %and_convert_fusion, s32[]{:T(128)} %constant.32.clone.1), window={size=1x1x128 pad=0_0x0_0x127_0}, to_apply=%region_3.4 | reduce-window | flops 130048 | bytes 8196 | tf_op jit(solution)/shard_map/reduce-window
  2.7 0.1 slice.8
  2.8 0.1 copy.7
  2.9 0.1 copy.8
  3.0 0.1 add_bitcast_fusion
  3.1 3.9 %convolution_convert_fusion = bf16[128,7168]{1,0:T(8,128)(2,1)} fusion(bf16[256,7168]{1,0:T(8,128)(2,1)} %param.6, s32[256]{0:T(256)S(1)} %multiply_add_fusion, pred[256]{0:T(512)(128)(4,1)S(1)} %reduce_or.9), kind=kOutput, calls=%fused_computation.2 | convolution fusion | flops 470745088 | bytes 5506304 | tf_op jit(solution)/shard_map/dot_general | solution.py:237
  7.1 103.6 %routed_experts.1 = bf16[4,2,16,7168]{3,2,1,0:T(8,128)(2,1)} custom-call(bf16[4,2,16,7168]{3,2,1,0:T(8,128)(2,1)} %bitcast.29, bf16[7168,256]{1,0:T(8,128)(2,1)} %bitcast.30, bf16[7168,256]{1,0:T(8,128)(2,1)} %bitcast.31, bf16[256,7168]{1,0:T(8,128)(2,1)} %bitcast.32), custom_call_target="tpu_custom_call" | custom-call | tf_op jit(solution)/shard_map/routed_experts/pallas_call | solution.py:179
  110.7 4.5 %fusion = bf16[256,7168]{1,0:T(8,128)(2,1)} fusion(bf16[128,7168]{1,0:T(8,128)(2,1)} %bitcast.28, f32[256]{0:T(256)S(1)} %get-tuple-element.5, s32[256]{0:T(256)S(1)} %multiply_add_fusion, pred[256]{0:T(512)(128)(4,1)S(1)} %reduce_or.9), kind=kOutput, calls=%fused_computation.1 | convolution fusion | flops 473497600 | bytes 5507328 | tf_op jit(solution)/shard_map/st,sd->td/dot_general | solution.py:243
  (6 shorter events, 0.1 us)

commit v2 on v1

--- a/solution.py
+++ b/solution.py
@@ -99,7 +99,7 @@
 
     def chunk_of(i):
         pair = i // 2
-        return 2 * (1 - pair % 2) + pair // 2, i % 2
+        return (1 - pair // 2) * (2 - pair) + (pair // 2) * 3 * (3 - pair), i % 2
 
     def finish(i):
         d, h = chunk_of(i)
@@ -227,9 +227,9 @@
     owners = jnp.sum(jnp.where(struck, routes // spacing, 0), axis=1)
     landed = jnp.any(struck, axis=1)
     weighting = jnp.sum(jnp.where(struck, route_gates, jnp.zeros_like(route_gates)), axis=1)
-    chosen = ((owners[:, None] == jnp.arange(groups)[None, :]) & landed[:, None]).astype(jnp.int32)
-    before = jnp.cumsum(chosen, axis=0) - chosen
-    ranking = jnp.sum(before * chosen, axis=1)
+    order = jnp.arange(token_count)
+    earlier = (owners[:, None] == owners[None, :]) & landed[:, None] & (order[:, None] < order[None, :])
+    ranking = jnp.sum(earlier.astype(jnp.int32), axis=0)
     target = owners * slot_count + ranking
     placing = (
         (jnp.arange(groups * slot_count)[:, None] == target[None, :]) & landed[None, :]
@@ -240,8 +240,11 @@
         returned = expert_call(outgoing, gate_proj, up_proj, down_proj)
     else:
         returned = plain_call(outgoing, gate_proj, up_proj, down_proj)
+    placed_back = (
+        (target[:, None] == jnp.arange(groups * slot_count)[None, :]) & landed[:, None]
+    ).astype(jnp.bfloat16)
     routed = jnp.einsum(
-        "st,sd->td", placing, returned.reshape(-1, model_width), preferred_element_type=jnp.float32
+        "ts,sd->td", placed_back, returned.reshape(-1, model_width), preferred_element_type=jnp.float32
     )
     return (weighting[:, None] * routed).astype(jnp.bfloat16)
 

time: 115 us -> 107 us (0.930)
  Pallas kernels: 104 us -> 96.8 us
  other arithmetic: 2.85 us -> 1.63 us
    pallas_call x1, Pallas kernels: 104 us -> 96.8 us  [expert_call(): pl.pallas_call(expert_kernel, out_shape=jax.ShapeDtypeStruct(halves, bf16...]
    another operation x2 -> x0, other arithmetic: 1.26 us -> none
where the time goes in v2:
time: 107 us
  Pallas kernels  96.8 us (90%)
  matrix products  8.42 us (8%)
  other arithmetic  1.63 us (2%)
    pallas_call x1, Pallas kernels, expert_call(): pl.pallas_call(expert_kernel, out_shape=jax.ShapeDtypeStruct(halves, bf16...  96.8 us
    dot_general x1, matrix products, on_device(): jnp.einsum('ts,sd->td', placed_back, returned.reshape(-1, model_width), p...  4.5 us
    dot_general x1, matrix products, on_device(): jnp.dot(placing, tokens, preferred_element_type=jnp.float32)  3.92 us

profile of v2, /device:TPU:0, one launch (start us, length us, event | category | flops | bytes accessed | tf_op | source)
XLA Modules:
  0.0 106.9 jit_solution(4589819179047093214)
XLA Ops:
  0.0 0.7 select_reduce_fusion
  0.8 0.7 fusion.12
  1.5 0.2 convert_reduce_fusion
  1.6 3.9 %convolution_convert_fusion = bf16[128,7168]{1,0:T(8,128)(2,1)} fusion(bf16[256,7168]{1,0:T(8,128)(2,1)} %param.6, s32[256]{0:T(256)S(1)} %multiply_add_fusion, pred[256]{0:T(512)(128)(4,1)S(1)} %reduce_or.9), kind=kOutput, calls=%fused_computation.2 | convolution fusion | flops 470745088 | bytes 5506304 | tf_op jit(solution)/shard_map/dot_general | solution.py:237
  5.6 96.8 %routed_experts.1 = bf16[4,2,16,7168]{3,2,1,0:T(8,128)(2,1)} custom-call(bf16[4,2,16,7168]{3,2,1,0:T(8,128)(2,1)} %bitcast.8, bf16[7168,256]{1,0:T(8,128)(2,1)} %bitcast.9, bf16[7168,256]{1,0:T(8,128)(2,1)} %bitcast.10, bf16[256,7168]{1,0:T(8,128)(2,1)} %bitcast.11), custom_call_target="tpu_custom_call" | custom-call | tf_op jit(solution)/shard_map/routed_experts/pallas_call | solution.py:179
  102.4 4.5 %fusion = bf16[256,7168]{1,0:T(8,128)(2,1)} fusion(bf16[128,7168]{1,0:T(8,128)(2,1)} %bitcast.7, f32[256]{0:T(256)S(1)} %get-tuple-element.5, s32[256]{0:T(256)S(1)} %multiply_add_fusion, pred[256]{0:T(512)(128)(4,1)S(1)} %reduce_or.9), kind=kOutput, calls=%fused_computation.1 | convolution fusion | flops 473497600 | bytes 5507328 | tf_op jit(solution)/shard_map/ts,sd->td/dot_general | solution.py:246
  (2 shorter events, 0.0 us)

commit v3 on v2

--- a/solution.py
+++ b/solution.py
@@ -35,8 +35,8 @@
 
 
 def expert_kernel(
-    outgoing, gate_hbm, up_hbm, down_hbm, returned,
-    gate_w, up_w, down_w, rows, kept, leaving, coming, summed,
+    tokens, placing, gate_hbm, up_hbm, down_hbm, returned,
+    outgoing, gate_w, up_w, down_w, rows, kept, leaving, coming, summed,
     local_sem, weight_send, weight_recv, zin_send, zin_recv, xin_send, xin_recv,
     xout_send, xout_recv, zout_send, zout_recv,
 ):
@@ -72,13 +72,29 @@
         low, high = d % 2, d // 2
         return z + low * (1 - 2 * (z % 2)) + high * (2 - 4 * ((z // 2) % 2))
 
-    for h in range(2):
-        zin(2, h).start()
-    for h in range(2):
-        rows[0, h, 0] = outgoing[z, h]
+    step = 1024
+
+    def gather(t, place):
+        picked = placing[t].reshape(2 * half_rows, placing.shape[3])
+
+        def one(n, carry):
+            columns = pl.ds(pl.multiple_of(n * step, step), step)
+            found = jnp.dot(picked, tokens[:, columns], preferred_element_type=jnp.float32)
+            found = found.astype(jnp.bfloat16)
+            for h in range(2):
+                place(h)[:, columns] = found[h * half_rows : (h + 1) * half_rows]
+            return carry
+
+        lax.fori_loop(0, width // step, one, 0)
+
+    gather(z, lambda h: rows.at[0, h, 0])
+    for h in range(2):
         xin(0, h).start()
-    for h in range(2):
-        zin(1, h).start()
+    for d in (2, 1):
+        t = swapped(z, d)
+        gather(t, lambda h: outgoing.at[t, h])
+        for h in range(2):
+            zin(d, h).start()
     weights = []
     for i, (hbm, vmem) in enumerate(((gate_hbm, gate_w), (up_hbm, up_w), (down_hbm, down_w))):
         own = pltpu.make_async_copy(hbm, vmem.at[0], local_sem.at[i])
@@ -86,6 +102,8 @@
         own.start()
         other.start()
         weights.append((own, other))
+    far = swapped(z, 3)
+    gather(far, lambda h: outgoing.at[far, h])
     for h in range(2):
         zin(2, h).wait_recv()
         xin(2, h).start()
@@ -130,8 +148,6 @@
             weights[2][0].wait()
             weights[2][1].wait_recv()
 
-        step = 1024
-
         def down(n, carry):
             columns = pl.ds(pl.multiple_of(n * step, step), step)
             part = jnp.dot(hidden[0], down_w[0, :, columns], preferred_element_type=jnp.float32)
@@ -169,8 +185,9 @@
                 zout(d, h, swapped(z, d)).wait()
 
 
-def expert_call(outgoing, gate_proj, up_proj, down_proj):
-    groups, slot_count, model_width = outgoing.shape
+def expert_call(tokens, placing, groups, gate_proj, up_proj, down_proj):
+    token_count, model_width = tokens.shape
+    slot_count = placing.shape[0] // groups
     hidden = gate_proj.shape[2]
     halves = (groups, 2, slot_count // 2, model_width)
     dma = pltpu.SemaphoreType.DMA
@@ -179,9 +196,10 @@
     returned = pl.pallas_call(
         expert_kernel,
         out_shape=jax.ShapeDtypeStruct(halves, bf16),
-        in_specs=[vmem, hbm, hbm, hbm],
+        in_specs=[vmem, vmem, hbm, hbm, hbm],
         out_specs=hbm,
         scratch_shapes=[
+            pltpu.VMEM(halves, bf16),
             pltpu.VMEM((2, model_width, hidden), bf16),
             pltpu.VMEM((2, model_width, hidden), bf16),
             pltpu.VMEM((2, hidden, model_width), bf16),
@@ -199,12 +217,15 @@
             collective_id=0, has_side_effects=True, vmem_limit_bytes=56 * 2**20
         ),
         name="routed_experts",
-    )(outgoing.reshape(halves), gate_proj[0], up_proj[0], down_proj[0])
+    )(tokens, placing.reshape(halves[:3] + (token_count,)), gate_proj[0], up_proj[0], down_proj[0])
     return returned.reshape(groups, slot_count, model_width)
 
 
-def plain_call(outgoing, gate_proj, up_proj, down_proj):
-    groups, slot_count, model_width = outgoing.shape
+def plain_call(tokens, placing, groups, gate_proj, up_proj, down_proj):
+    model_width = tokens.shape[1]
+    slot_count = placing.shape[0] // groups
+    outgoing = jnp.dot(placing, tokens, preferred_element_type=jnp.float32).astype(jnp.bfloat16)
+    outgoing = outgoing.reshape(groups, slot_count, model_width)
     arrived = lax.all_to_all(outgoing, "grp", split_axis=0, concat_axis=0, tiled=True)
     weight_set = (
         lax.all_gather(gate_proj, "dp", axis=2, tiled=True),
@@ -234,12 +255,10 @@
     placing = (
         (jnp.arange(groups * slot_count)[:, None] == target[None, :]) & landed[None, :]
     ).astype(jnp.bfloat16)
-    outgoing = jnp.dot(placing, tokens, preferred_element_type=jnp.float32).astype(jnp.bfloat16)
-    outgoing = outgoing.reshape(groups, slot_count, model_width)
     if groups == 4 and lax.axis_size("ing") == 2 and lax.axis_size("dp") == 2 and slot_count == 32:
-        returned = expert_call(outgoing, gate_proj, up_proj, down_proj)
+        returned = expert_call(tokens, placing, groups, gate_proj, up_proj, down_proj)
     else:
-        returned = plain_call(outgoing, gate_proj, up_proj, down_proj)
+        returned = plain_call(tokens, placing, groups, gate_proj, up_proj, down_proj)
     placed_back = (
         (target[:, None] == jnp.arange(groups * slot_count)[None, :]) & landed[:, None]
     ).astype(jnp.bfloat16)

time: 107 us -> 114 us (1.065)
  Pallas kernels: 96.8 us -> 106 us
  matrix products: 8.42 us -> 4.51 us
    pallas_call x1, Pallas kernels: 96.8 us -> 106 us  [expert_call(): pl.pallas_call(expert_kernel, out_shape=jax.ShapeDtypeStruct(halves, bf16...]
    dot_general x1 -> x0, matrix products: 3.92 us -> none  [on_device(): jnp.dot(placing, tokens, preferred_element_type=jnp.float32)]
where the time goes in v3:
time: 114 us; the launch traced here: 113 us
  Pallas kernels  106 us (93%)
  matrix products  4.51 us (4%)
  other arithmetic  2.36 us (2%)
    pallas_call x1, Pallas kernels, expert_call(): pl.pallas_call(expert_kernel, out_shape=jax.ShapeDtypeStruct(halves, bf16...  106 us
    dot_general x1, matrix products, on_device(): jnp.einsum('ts,sd->td', placed_back, returned.reshape(-1, model_width), p...  4.51 us

profile of v3, /device:TPU:0, one launch (start us, length us, event | category | flops | bytes accessed | tf_op | source)
XLA Modules:
  0.0 113.3 jit_solution(802085422883605508)
XLA Ops:
  0.0 0.7 select_reduce_fusion
  0.8 0.7 fusion.8
  1.5 0.2 convert_reduce_fusion
  1.7 0.7 and_convert_fusion.placing
  2.4 106.4 %routed_experts.1 = bf16[4,2,16,7168]{3,2,1,0:T(8,128)(2,1)} custom-call(bf16[256,7168]{1,0:T(8,128)(2,1)} %tokens.1, bf16[4,2,16,256]{3,2,1,0:T(8,128)(2,1)} %and_convert_fusion.placing, bf16[7168,256]{1,0:T(8,128)(2,1)} %bitcast.6, bf16[7168,256]{1,0:T(8,128)(2,1)} %bitcast.7, bf16[256,7168]{1,0:T(8,128)(2,1)} %bitcast.8), custom_call_target="tpu_custom_call" | custom-call | tf_op jit(solution)/shard_map/routed_experts/pallas_call | solution.py:196
  108.8 4.5 %fusion = bf16[256,7168]{1,0:T(8,128)(2,1)} fusion(bf16[128,7168]{1,0:T(8,128)(2,1)} %bitcast.5, f32[256]{0:T(256)S(1)} %get-tuple-element.5, s32[256]{0:T(256)S(1)} %multiply_add_fusion.1, pred[256]{0:T(512)(128)(4,1)S(1)} %reduce_or.9), kind=kOutput, calls=%fused_computation.1 | convolution fusion | flops 473497600 | bytes 5507328 | tf_op jit(solution)/shard_map/ts,sd->td/dot_general | solution.py:265
  (3 shorter events, 0.0 us)

commit v4 on v2

--- a/solution.py
+++ b/solution.py
@@ -97,35 +97,35 @@
         own.wait()
         other.wait_recv()
 
-    def chunk_of(i):
-        pair = i // 2
-        return (1 - pair // 2) * (2 - pair) + (pair // 2) * 3 * (3 - pair), i % 2
-
-    def finish(i):
-        d, h = chunk_of(i)
-        xout(d, h).wait_recv()
-        summed[d, h] = (kept[d, h] + coming[d, h].astype(jnp.float32)).astype(jnp.bfloat16)
-
-        @pl.when(d == 0)
-        def _():
-            pltpu.make_async_copy(summed.at[d, h], returned.at[z, h], local_sem.at[3 + h]).start()
-
-        @pl.when(d != 0)
-        def _():
-            zout(d, h, flipped(d)).start()
-
-    def compute(i, carry):
-        d, h = chunk_of(i)
-        xin(d, h).wait_recv()
-        chunk = rows.at[d, h]
-        tile = chunk[...].reshape(2 * half_rows, width)
+    def distance(p):
+        return (1 - p // 2) * (2 - p) + (p // 2) * 3 * (3 - p)
+
+    def finish(p):
+        d = distance(p)
+        for h in range(2):
+            xout(d, h).wait_recv()
+            summed[d, h] = (kept[d, h] + coming[d, h].astype(jnp.float32)).astype(jnp.bfloat16)
+
+            @pl.when(d == 0)
+            def _():
+                pltpu.make_async_copy(summed.at[d, h], returned.at[z, h], local_sem.at[3 + h]).start()
+
+            @pl.when(d != 0)
+            def _():
+                zout(d, h, flipped(d)).start()
+
+    def compute(p, carry):
+        d = distance(p)
+        for h in range(2):
+            xin(d, h).wait_recv()
+        tile = rows[d].reshape(4 * half_rows, width)
         hidden = []
         for w in range(2):
             gate_act = jnp.dot(tile, gate_w[w], preferred_element_type=jnp.float32)
             up_act = jnp.dot(tile, up_w[w], preferred_element_type=jnp.float32)
             hidden.append((gate_act / (1.0 + jnp.exp(-gate_act)) * up_act).astype(jnp.bfloat16))
 
-        @pl.when(i == 0)
+        @pl.when(p == 0)
         def _():
             weights[2][0].wait()
             weights[2][1].wait_recv()
@@ -136,27 +136,29 @@
             columns = pl.ds(pl.multiple_of(n * step, step), step)
             part = jnp.dot(hidden[0], down_w[0, :, columns], preferred_element_type=jnp.float32)
             part += jnp.dot(hidden[1], down_w[1, :, columns], preferred_element_type=jnp.float32)
-            kept[d, h, :, columns] = part[:half_rows]
-            leaving[d, h, :, columns] = part[half_rows:].astype(jnp.bfloat16)
+            for h in range(2):
+                mine, theirs = 2 * h * half_rows, (2 * h + 1) * half_rows
+                kept[d, h, :, columns] = part[mine : mine + half_rows]
+                leaving[d, h, :, columns] = part[theirs : theirs + half_rows].astype(jnp.bfloat16)
             return carry
 
         lax.fori_loop(0, width // step, down, 0)
-        xout(d, h).start()
-
-        @pl.when((i == 1) | (i == 3))
+        for h in range(2):
+            xout(d, h).start()
+
+        @pl.when(p < 2)
         def _():
-            zin(3, i // 2).wait_recv()
-            xin(3, i // 2).start()
-
-        @pl.when(i >= 2)
+            zin(3, p).wait_recv()
+            xin(3, p).start()
+
+        @pl.when(p >= 1)
         def _():
-            finish(i - 2)
+            finish(p - 1)
 
         return carry
 
-    lax.fori_loop(0, 8, compute, 0)
-    for i in (6, 7):
-        finish(i)
+    lax.fori_loop(0, 4, compute, 0)
+    finish(3)
     for own, other in weights:
         other.wait_send()
     for h in range(2):

time: 107 us -> 108 us (level)
  Pallas kernels: 96.8 us -> 98 us
    pallas_call x1, Pallas kernels: 96.8 us -> 98 us  [expert_call(): pl.pallas_call(expert_kernel, out_shape=jax.ShapeDtypeStruct(halves, bf16...]
where the time goes in v4:
time: 108 us
  Pallas kernels  98 us (91%)
  matrix products  8.42 us (8%)
  other arithmetic  1.63 us (2%)
    pallas_call x1, Pallas kernels, expert_call(): pl.pallas_call(expert_kernel, out_shape=jax.ShapeDtypeStruct(halves, bf16...  98 us
    dot_general x1, matrix products, on_device(): jnp.einsum('ts,sd->td', placed_back, returned.reshape(-1, model_width), p...  4.5 us
    dot_general x1, matrix products, on_device(): jnp.dot(placing, tokens, preferred_element_type=jnp.float32)  3.92 us

profile of v4, /device:TPU:0, one launch (start us, length us, event | category | flops | bytes accessed | tf_op | source)
XLA Modules:
  0.0 108.1 jit_solution(7674019980118399017)
XLA Ops:
  0.0 0.7 select_reduce_fusion
  0.8 0.7 fusion.12
  1.5 0.2 convert_reduce_fusion
  1.6 3.9 %convolution_convert_fusion = bf16[128,7168]{1,0:T(8,128)(2,1)} fusion(bf16[256,7168]{1,0:T(8,128)(2,1)} %param.6, s32[256]{0:T(256)S(1)} %multiply_add_fusion, pred[256]{0:T(512)(128)(4,1)S(1)} %reduce_or.9), kind=kOutput, calls=%fused_computation.2 | convolution fusion | flops 470745088 | bytes 5506304 | tf_op jit(solution)/shard_map/dot_general | solution.py:239
  5.6 98.0 %routed_experts.1 = bf16[4,2,16,7168]{3,2,1,0:T(8,128)(2,1)} custom-call(bf16[4,2,16,7168]{3,2,1,0:T(8,128)(2,1)} %bitcast.8, bf16[7168,256]{1,0:T(8,128)(2,1)} %bitcast.9, bf16[7168,256]{1,0:T(8,128)(2,1)} %bitcast.10, bf16[256,7168]{1,0:T(8,128)(2,1)} %bitcast.11), custom_call_target="tpu_custom_call" | custom-call | tf_op jit(solution)/shard_map/routed_experts/pallas_call | solution.py:181
  103.6 4.5 %fusion = bf16[256,7168]{1,0:T(8,128)(2,1)} fusion(bf16[128,7168]{1,0:T(8,128)(2,1)} %bitcast.7, f32[256]{0:T(256)S(1)} %get-tuple-element.5, s32[256]{0:T(256)S(1)} %multiply_add_fusion, pred[256]{0:T(512)(128)(4,1)S(1)} %reduce_or.9), kind=kOutput, calls=%fused_computation.1 | convolution fusion | flops 473497600 | bytes 5507328 | tf_op jit(solution)/shard_map/ts,sd->td/dot_general | solution.py:248
  (2 shorter events, 0.0 us)

commit v5 on v2

--- a/solution.py
+++ b/solution.py
@@ -72,13 +72,6 @@
         low, high = d % 2, d // 2
         return z + low * (1 - 2 * (z % 2)) + high * (2 - 4 * ((z // 2) % 2))
 
-    for h in range(2):
-        zin(2, h).start()
-    for h in range(2):
-        rows[0, h, 0] = outgoing[z, h]
-        xin(0, h).start()
-    for h in range(2):
-        zin(1, h).start()
     weights = []
     for i, (hbm, vmem) in enumerate(((gate_hbm, gate_w), (up_hbm, up_w), (down_hbm, down_w))):
         own = pltpu.make_async_copy(hbm, vmem.at[0], local_sem.at[i])
@@ -87,19 +80,26 @@
         other.start()
         weights.append((own, other))
     for h in range(2):
+        zin(1, h).start()
+    for h in range(2):
+        zin(2, h).start()
+    for h in range(2):
+        rows[0, h, 0] = outgoing[z, h]
+        xin(0, h).start()
+    for h in range(2):
+        zin(1, h).wait_recv()
+        xin(1, h).start()
+    for h in range(2):
         zin(2, h).wait_recv()
         xin(2, h).start()
         zin(3, h).start()
-    for h in range(2):
-        zin(1, h).wait_recv()
-        xin(1, h).start()
     for own, other in weights[:2]:
         own.wait()
         other.wait_recv()
 
     def chunk_of(i):
         pair = i // 2
-        return (1 - pair // 2) * (2 - pair) + (pair // 2) * 3 * (3 - pair), i % 2
+        return (pair + 1) % 4, i % 2
 
     def finish(i):
         d, h = chunk_of(i)

time: 107 us -> 111 us (1.037)
  the two profiles are of different devices: /device:TPU:0 before, /device:TPU:8 now
where the time goes in v5:
time: 111 us
  Pallas kernels  101 us (91%)
  matrix products  8.43 us (8%)
  other arithmetic  1.63 us (1%)
    pallas_call x1, Pallas kernels, expert_call(): pl.pallas_call(expert_kernel, out_shape=jax.ShapeDtypeStruct(halves, bf16...  101 us
    dot_general x1, matrix products, on_device(): jnp.einsum('ts,sd->td', placed_back, returned.reshape(-1, model_width), p...  4.5 us
    dot_general x1, matrix products, on_device(): jnp.dot(placing, tokens, preferred_element_type=jnp.float32)  3.92 us

profile of v5, /device:TPU:8, one launch (start us, length us, event | category | flops | bytes accessed | tf_op | source)
XLA Modules:
  0.0 110.8 jit_solution(7603184654153621577)
XLA Ops:
  0.0 0.7 select_reduce_fusion
  0.8 0.7 fusion.12
  1.5 0.2 convert_reduce_fusion
  1.6 3.9 %convolution_convert_fusion = bf16[128,7168]{1,0:T(8,128)(2,1)} fusion(bf16[256,7168]{1,0:T(8,128)(2,1)} %param.6, s32[256]{0:T(256)S(1)} %multiply_add_fusion, pred[256]{0:T(512)(128)(4,1)S(1)} %reduce_or.9), kind=kOutput, calls=%fused_computation.2 | convolution fusion | flops 470745088 | bytes 5506304 | tf_op jit(solution)/shard_map/dot_general | solution.py:237
  5.6 100.7 %routed_experts.1 = bf16[4,2,16,7168]{3,2,1,0:T(8,128)(2,1)} custom-call(bf16[4,2,16,7168]{3,2,1,0:T(8,128)(2,1)} %bitcast.8, bf16[7168,256]{1,0:T(8,128)(2,1)} %bitcast.9, bf16[7168,256]{1,0:T(8,128)(2,1)} %bitcast.10, bf16[256,7168]{1,0:T(8,128)(2,1)} %bitcast.11), custom_call_target="tpu_custom_call" | custom-call | tf_op jit(solution)/shard_map/routed_experts/pallas_call | solution.py:179
  106.3 4.5 %fusion = bf16[256,7168]{1,0:T(8,128)(2,1)} fusion(bf16[128,7168]{1,0:T(8,128)(2,1)} %bitcast.7, f32[256]{0:T(256)S(1)} %get-tuple-element.5, s32[256]{0:T(256)S(1)} %multiply_add_fusion, pred[256]{0:T(512)(128)(4,1)S(1)} %reduce_or.9), kind=kOutput, calls=%fused_computation.1 | convolution fusion | flops 473497600 | bytes 5507328 | tf_op jit(solution)/shard_map/ts,sd->td/dot_general | solution.py:246
  (2 shorter events, 0.0 us)
